TPU v7x, 32 devices: a whole 2x2x4 slice. The times are simulated.
32 devices in a mesh: groups: 2 (over x), query: 16 (over z, y, core).
Axes of the slice: x: 2, y: 2, z: 4, core: 2. Of those that a mesh axis runs over, the one named last changes fastest.
Arguments:
- tokens: bfloat16 [384, 4096], P(('groups', 'query')), parts along dimension 0, may hold values from -6 to 6
- grad_out: bfloat16 [384, 4096], P(('groups', 'query')), parts along dimension 0, may hold values from -6 to 6
- gate_weight: bfloat16 [4096, 14336], P(None, 'query'), may hold values from -0.09375 to 0.09375
- up_weight: bfloat16 [4096, 14336], P(None, 'query'), may hold values from -0.09375 to 0.09375
- query_left: bfloat16 [16, 4096, 32], P('query'), may hold values from -0.09375 to 0.09375
- query_right: bfloat16 [16, 14336, 32], P('query'), may hold values from -0.09375 to 0.09375
Outputs:
- scores: float32 [384, 16], P(('groups', 'query')), parts along dimension 0
There are 2 independent parts, one for each index of `groups`. A program takes and returns all parts, laid end to end along the dimension named above; an argument that names none is the same for every part. Nothing has to cross between parts.
All inputs are finite; a program needn't handle non-finite values.
Results may differ from a plain program's by a relative error of at most 0.0003.
Values may be sent and summed in bfloat16 or wider, within the bound.
No kernel may reach another device: no remote copies, remote signals or barrier semaphores. Data moves between devices by JAX's collectives and lax.ppermute only.
A program may use at most 128 MiB of HBM per device.

v0:
```python
import jax
import jax.numpy as jnp
from jax import lax
from jax.sharding import PartitionSpec as P

AXIS = "query"
F32 = jnp.float32
BF16 = jnp.bfloat16


def swap(x, bit):
    n = lax.axis_size(AXIS)
    return lax.ppermute(x, AXIS, [(i, i ^ bit) for i in range(n)])


def pick(flag, when_zero, when_one):
    return jnp.where(flag == 0, when_zero, when_one)


def z_order(planes):
    order = [0]
    bit = planes // 2
    while bit >= 1:
        order = order + [k | bit for k in order]
        bit //= 2
    return order


def gather_rows(rows, core, planes):
    half = rows.shape[1] // 2
    mine = pick(core, rows[:, :half], rows[:, half:])
    theirs = pick(core, rows[:, half:], rows[:, :half])
    other = swap(theirs, 1)
    chip = pick(core, jnp.concatenate([mine, other]), jnp.concatenate([other, mine]))
    column = jnp.concatenate([chip if k == 0 else swap(chip, 4 * k) for k in z_order(planes)])
    both = jnp.concatenate([column, swap(column, 2)])
    rest = swap(both, 1)
    return pick(core, jnp.concatenate([both, rest], 1), jnp.concatenate([rest, both], 1))


def body(tokens, grad_out, gate_weight, up_weight, query_left, query_right):
    n = lax.axis_size(AXIS)
    planes = n // 4
    here = lax.axis_index(AXIS)
    core, y, z = (here & 1, here >> 1 & 1, here >> 2)
    rank = query_right.shape[2]
    cols = gate_weight.shape[1]
    blocks = query_right[0].T.reshape(rank, n, cols).transpose(1, 0, 2)
    factors = lax.all_to_all(blocks, AXIS, split_axis=0, concat_axis=0, tiled=True)
    factors = factors.reshape(n // 2, 2, rank, cols)
    keep_factors = pick(core, factors[:, 0], factors[:, 1]).reshape(n // 2 * rank, cols)
    send_factors = pick(core, factors[:, 1], factors[:, 0]).reshape(n // 2 * rank, cols)
    whole = gather_rows(tokens, core, planes)
    grads = gather_rows(grad_out, core, planes)
    gate = jnp.dot(whole, gate_weight, preferred_element_type=F32)
    up = jnp.dot(whole, up_weight, preferred_element_type=F32)
    hidden = jax.nn.silu(gate) * up
    head = lax.reduce_precision(hidden, exponent_bits=8, mantissa_bits=7)
    high = head.astype(BF16)
    low = (hidden - head).astype(BF16)

    def project(with_factors):
        dims = (((1,), (1,)), ((), ()))
        return lax.dot_general(
            high, with_factors, dims, preferred_element_type=F32
        ) + lax.dot_general(low, with_factors, dims, preferred_element_type=F32)

    left = jnp.dot(grads, query_left[0], preferred_element_type=F32)
    right = project(keep_factors) + swap(project(send_factors), 1)
    bit, place = (2, y)
    while bit < n:
        half = right.shape[0] // 2
        right = right[:half] + swap(right[half:], bit)
        other = swap(left[half:], bit)
        left = pick(
            place,
            jnp.concatenate([left[:half], other], 1),
            jnp.concatenate([other, left[:half]], 1),
        )
        bit *= 2
        place = here // bit & 1
    own = tokens.shape[0]
    spread = lax.broadcasted_iota(jnp.int32, (n // 2 * rank, n), 0) // rank * 2 + core
    spread = (spread == lax.broadcasted_iota(jnp.int32, (n // 2 * rank, n), 1)).astype(F32)
    sums = jnp.dot(left * right, spread, precision=lax.Precision.HIGHEST)
    return pick(core, sums[:own], sums[own:]) + swap(pick(core, sums[own:], sums[:own]), 1)


def solution(mesh):
    return jax.shard_map(
        body,
        mesh=mesh,
        in_specs=(
            P(("groups", "query"), None),
            P(("groups", "query"), None),
            P(None, "query"),
            P(None, "query"),
            P("query", None, None),
            P("query", None, None),
        ),
        out_specs=P(("groups", "query"), None),
        check_vma=False,
    )
```

profile of v0, /device:TPU:0, one launch (start us, length us, event | category | flops | bytes accessed | tf_op | source)
XLA Modules:
  0.0 86.0 jit_solution(18113915444369536713)
XLA Ops:
  0.0 1.0 %broadcast_select_fusion.4 = (bf16[12,2048]{1,0:T(8,128)(2,1)S(1)}, bf16[12,2048]{1,0:T(8,128)(2,1)S(1)}) fusion(pred[]{:T(512)S(6)} %eq.10, bf16[12,4096]{1,0:T(8,128)(2,1)} %param.7), kind=kLoop, calls=%fused_computation.37 | loop fusion | flops 49152 | bytes 196609 | tf_op jit(solution)/shard_map/jit(_where)/select_n | solution.py:17
  1.0 0.5 collective-permute-start
  1.5 0.9 %broadcast_select_fusion.2 = (bf16[12,2048]{1,0:T(8,128)(2,1)S(1)}, bf16[12,2048]{1,0:T(8,128)(2,1)S(1)}) fusion(pred[]{:T(512)S(6)} %eq.10, bf16[12,4096]{1,0:T(8,128)(2,1)} %param.6), kind=kLoop, calls=%fused_computation.35 | loop fusion | flops 49152 | bytes 196609 | tf_op jit(solution)/shard_map/jit(_where)/select_n | solution.py:17
  2.6 4.1 %collective-permute-start.1 = (bf16[24,2048]{1,0:T(8,128)(2,1)S(1)}, bf16[24,2048]{1,0:T(8,128)(2,1)S(1)}, u32[]{:S(2)}, u32[]{:S(2)}) collective-permute-start(bf16[24,2048]{1,0:T(8,128)(2,1)S(1)} %get-tuple-element.6), channel_id=1, source_target_pairs={{0,8},{1,9},{2,10},{3,11},{4,12},{5,13},{6,14},{7,15},{8,0},{9,1},... | collective-permute-start | bytes 294920 | tf_op jit(solution)/shard_map/ppermute | solution.py:13
  6.7 1.6 %collective-permute-start.2 = (bf16[24,2048]{1,0:T(8,128)(2,1)S(1)}, bf16[24,2048]{1,0:T(8,128)(2,1)S(1)}, u32[]{:S(2)}, u32[]{:S(2)}) collective-permute-start(bf16[24,2048]{1,0:T(8,128)(2,1)S(1)} %get-tuple-element.6), channel_id=1, source_target_pairs={{0,4},{1,5},{2,6},{3,7},{4,0},{5,1},{6,2},{7,3},{8,12},{9,13},{10,... | collective-permute-start | bytes 294920 | tf_op jit(solution)/shard_map/ppermute | solution.py:13
  8.3 2.0 %collective-permute-start.10 = (bf16[24,2048]{1,0:T(8,128)(2,1)S(1)}, bf16[24,2048]{1,0:T(8,128)(2,1)S(1)}, u32[]{:S(2)}, u32[]{:S(2)}) collective-permute-start(bf16[24,2048]{1,0:T(8,128)(2,1)S(1)} %get-tuple-element.8), channel_id=1, source_target_pairs={{0,8},{1,9},{2,10},{3,11},{4,12},{5,13},{6,14},{7,15},{8,0},{9,1},... | collective-permute-start | bytes 294920 | tf_op jit(solution)/shard_map/ppermute | solution.py:13
  10.3 2.5 %collective-permute-start.11 = (bf16[24,2048]{1,0:T(8,128)(2,1)S(1)}, bf16[24,2048]{1,0:T(8,128)(2,1)S(1)}, u32[]{:S(2)}, u32[]{:S(2)}) collective-permute-start(bf16[24,2048]{1,0:T(8,128)(2,1)S(1)} %get-tuple-element.8), channel_id=1, source_target_pairs={{0,4},{1,5},{2,6},{3,7},{4,0},{5,1},{6,2},{7,3},{8,12},{9,13},{10,... | collective-permute-start | bytes 294920 | tf_op jit(solution)/shard_map/ppermute | solution.py:13
  12.8 6.2 %collective-permute-start.12 = (bf16[24,2048]{1,0:T(8,128)(2,1)S(1)}, bf16[24,2048]{1,0:T(8,128)(2,1)S(1)}, u32[]{:S(2)}, u32[]{:S(2)}) collective-permute-start(bf16[24,2048]{1,0:T(8,128)(2,1)S(1)} %get-tuple-element.8), channel_id=1, source_target_pairs={{0,12},{1,13},{2,14},{3,15},{4,8},{5,9},{6,10},{7,11},{8,4},{9,5},... | collective-permute-start | bytes 294920 | tf_op jit(solution)/shard_map/ppermute | solution.py:13
  19.0 1.6 %collective-permute-start.4 = (bf16[96,2048]{1,0:T(8,128)(2,1)S(1)}, bf16[96,2048]{1,0:T(8,128)(2,1)S(1)}, u32[]{:S(2)}, u32[]{:S(2)}) collective-permute-start(bf16[96,2048]{1,0:T(8,128)(2,1)S(1)} %pad_maximum_fusion), channel_id=1, source_target_pairs={{0,2},{1,3},{2,0},{3,1},{4,6},{5,7},{6,4},{7,5},{8,10},{9,11},{10,... | collective-permute-start | bytes 1179656 | tf_op jit(solution)/shard_map/ppermute | solution.py:13
  20.6 2.3 %collective-permute-done.10 = bf16[24,2048]{1,0:T(8,128)(2,1)S(1)} collective-permute-done((bf16[24,2048]{1,0:T(8,128)(2,1)S(1)}, bf16[24,2048]{1,0:T(8,128)(2,1)S(1)}, u32[]{:S(2)}, u32[]{:S(2)}) %collective-permute-start.10) | collective-permute-done | bytes 98336 | tf_op jit(solution)/shard_map/ppermute | solution.py:13
  23.0 1.9 %collective-permute-start.13 = (bf16[96,2048]{1,0:T(8,128)(2,1)S(1)}, bf16[96,2048]{1,0:T(8,128)(2,1)S(1)}, u32[]{:S(2)}, u32[]{:S(2)}) collective-permute-start(bf16[96,2048]{1,0:T(8,128)(2,1)S(1)} %pad_maximum_fusion.1), channel_id=1, source_target_pairs={{0,2},{1,3},{2,0},{3,1},{4,6},{5,7},{6,4},{7,5},{8,10},{9,11},{10,... | collective-permute-start | bytes 1179656 | tf_op jit(solution)/shard_map/ppermute | solution.py:13
  24.9 4.9 %collective-permute-done.4 = bf16[96,2048]{1,0:T(8,128)(2,1)S(1)} collective-permute-done((bf16[96,2048]{1,0:T(8,128)(2,1)S(1)}, bf16[96,2048]{1,0:T(8,128)(2,1)S(1)}, u32[]{:S(2)}, u32[]{:S(2)}) %collective-permute-start.4) | collective-permute-done | bytes 393248 | tf_op jit(solution)/shard_map/ppermute | solution.py:13
  29.9 5.5 %collective-permute-done.13 = bf16[96,2048]{1,0:T(8,128)(2,1)S(1)} collective-permute-done((bf16[96,2048]{1,0:T(8,128)(2,1)S(1)}, bf16[96,2048]{1,0:T(8,128)(2,1)S(1)}, u32[]{:S(2)}, u32[]{:S(2)}) %collective-permute-start.13) | collective-permute-done | bytes 393248 | tf_op jit(solution)/shard_map/ppermute | solution.py:13
  35.6 1.1 %copy.32 = bf16[16,32,896]{2,1,0:T(8,128)(2,1)} copy(bf16[16,32,896]{2,0,1:T(8,128)(2,1)S(1)} %bitcast.23) | data formatting | bytes 1835008 | tf_op jit(solution)/shard_map/transpose | solution.py:48
  36.7 8.1 %all-to-all-start = ((bf16[16,32,896]{2,1,0:T(8,128)(2,1)}), bf16[16,32,896]{2,1,0:T(8,128)(2,1)S(1)}, u32[]{:S(2)}, u32[]{:S(2)}) async-start(bf16[16,32,896]{2,1,0:T(8,128)(2,1)} %copy.32), calls=%async_computation | async-start | bytes 1835008 | tf_op jit(solution)/shard_map/all_to_all | solution.py:49
  44.9 2.0 %fusion = f32[192,32]{0,1:T(8,128)S(1)} fusion(bf16[192,2048]{1,0:T(8,128)(2,1)} %collective-permute-done.5, bf16[192,2048]{1,0:T(8,128)(2,1)S(1)} %constant_dynamic-update-slice_fusion, pred[]{:T(512)S(6)} %eq.10, bf16[1,4096,32]{1,2,0:T(8,128)(2,1)S(1)} %copy-done), kind=kOutput, calls=%fused_computation.1 | convolution fusion | flops 57409536 | bytes 1859585 | tf_op jit(solution)/shard_map/dot_general | solution.py:68
  47.0 1.9 %collective-permute-start.6 = (f32[96,32]{0,1:T(8,128)S(1)}, f32[96,32]{0,1:T(8,128)S(1)}, u32[]{:S(2)}, u32[]{:S(2)}) collective-permute-start(f32[96,32]{0,1:T(8,128)S(1)} %get-tuple-element.18), channel_id=1, source_target_pairs={{0,2},{1,3},{2,0},{3,1},{4,6},{5,7},{6,4},{7,5},{8,10},{9,11},{10,... | collective-permute-start | bytes 36872 | tf_op jit(solution)/shard_map/ppermute | solution.py:13
  48.9 5.2 %fusion.10 = f32[192,896]{1,0:T(8,128)S(1)} fusion(bf16[4096,896]{1,0:T(8,128)(2,1)} %param.8, bf16[192,2048]{1,0:T(8,128)(2,1)S(1)} %collective-permute-done.14, bf16[192,2048]{1,0:T(8,128)(2,1)S(1)} %constant_dynamic-update-slice_fusion.5, pred[]{:T(512)S(6)} %eq.10), kind=kOutput, calls=%fused_computation.21 | convolution fusion | flops 1416364032 | bytes 9601025 | tf_op jit(solution)/shard_map/dot_general | solution.py:55
  54.2 1.9 %collective-permute-start.7 = (f32[48,64]{0,1:T(8,128)S(1)}, f32[48,64]{0,1:T(8,128)S(1)}, u32[]{:S(2)}, u32[]{:S(2)}) collective-permute-start(f32[48,64]{0,1:T(8,128)S(1)} %get-tuple-element.16), channel_id=1, source_target_pairs={{0,4},{1,5},{2,6},{3,7},{4,0},{5,1},{6,2},{7,3},{8,12},{9,13},{10,... | collective-permute-start | bytes 36872 | tf_op jit(solution)/shard_map/ppermute | solution.py:13
  56.1 1.9 %multiply_multiply_fusion = f32[192,896]{1,0:T(8,128)S(1)} fusion(f32[192,896]{1,0:T(8,128)S(1)} %fusion.10, bf16[4096,896]{1,0:T(8,128)(2,1)S(1)} %bitcast.27, bf16[192,2048]{1,0:T(8,128)(2,1)S(1)} %collective-permute-done.14, bf16[192,2048]{1,0:T(8,128)(2,1)S(1)} %constant_dynamic-update-slice_fusion.5, pred[]{:T(512)S(6)} %eq.10), kind=kOutput, calls=%fused_computation.15 | convolution fusion | flops 1417224192 | bytes 10289153 | tf_op jit(solution)/shard_map/dot_general | solution.py:56
  58.0 3.4 %collective-permute-done.7 = f32[48,64]{0,1:T(8,128)S(1)} collective-permute-done((f32[48,64]{0,1:T(8,128)S(1)}, f32[48,64]{0,1:T(8,128)S(1)}, u32[]{:S(2)}, u32[]{:S(2)}) %collective-permute-start.7) | collective-permute-done | bytes 12320 | tf_op jit(solution)/shard_map/ppermute | solution.py:13
  61.5 4.4 %all-to-all-done = bf16[16,32,896]{2,1,0:T(8,128)(2,1)S(1)} async-done(((bf16[16,32,896]{2,1,0:T(8,128)(2,1)}), bf16[16,32,896]{2,1,0:T(8,128)(2,1)S(1)}, u32[]{:S(2)}, u32[]{:S(2)}) %all-to-all-start) | async-done | bytes 917536 | tf_op jit(solution)/shard_map/all_to_all | solution.py:49
  67.2 0.9 %collective-permute-done.15 = f32[192,256]{1,0:T(8,128)S(1)} collective-permute-done((f32[192,256]{1,0:T(8,128)S(1)}, f32[192,256]{1,0:T(8,128)S(1)}, u32[]{:S(2)}, u32[]{:S(2)}) %collective-permute-start.15) | collective-permute-done | bytes 196640 | tf_op jit(solution)/shard_map/ppermute | solution.py:13
  68.5 1.7 %collective-permute-start.16 = (f32[96,256]{1,0:T(8,128)S(1)}, f32[96,256]{1,0:T(8,128)S(1)}, u32[]{:S(2)}, u32[]{:S(2)}) collective-permute-start(f32[96,256]{1,0:T(8,128)S(1)} %slice.100), channel_id=1, source_target_pairs={{0,2},{1,3},{2,0},{3,1},{4,6},{5,7},{6,4},{7,5},{8,10},{9,11},{10,... | collective-permute-start | bytes 294920 | tf_op jit(solution)/shard_map/ppermute | solution.py:13
  70.3 3.2 %collective-permute-done.16 = f32[96,256]{1,0:T(8,128)S(1)} collective-permute-done((f32[96,256]{1,0:T(8,128)S(1)}, f32[96,256]{1,0:T(8,128)S(1)}, u32[]{:S(2)}, u32[]{:S(2)}) %collective-permute-start.16) | collective-permute-done | bytes 98336 | tf_op jit(solution)/shard_map/ppermute | solution.py:13
  73.6 3.0 %collective-permute-start.17 = (f32[48,256]{1,0:T(8,128)S(1)}, f32[48,256]{1,0:T(8,128)S(1)}, u32[]{:S(2)}, u32[]{:S(2)}) collective-permute-start(f32[48,256]{1,0:T(8,128)S(1)} %slice.102), channel_id=1, source_target_pairs={{0,4},{1,5},{2,6},{3,7},{4,0},{5,1},{6,2},{7,3},{8,12},{9,13},{10,... | collective-permute-start | bytes 147464 | tf_op jit(solution)/shard_map/ppermute | solution.py:13
  76.6 1.2 %collective-permute-start.8 = (f32[24,128]{1,0:T(8,128)S(1)}, f32[24,128]{1,0:T(8,128)S(1)}, u32[]{:S(2)}, u32[]{:S(2)}) collective-permute-start(f32[24,128]{1,0:T(8,128)S(1)} %get-tuple-element.20), channel_id=1, source_target_pairs={{0,8},{1,9},{2,10},{3,11},{4,12},{5,13},{6,14},{7,15},{8,0},{9,1},... | collective-permute-start | bytes 36872 | tf_op jit(solution)/shard_map/ppermute | solution.py:13
  77.8 0.9 %collective-permute-done.17 = f32[48,256]{1,0:T(8,128)S(1)} collective-permute-done((f32[48,256]{1,0:T(8,128)S(1)}, f32[48,256]{1,0:T(8,128)S(1)}, u32[]{:S(2)}, u32[]{:S(2)}) %collective-permute-start.17) | collective-permute-done | bytes 49184 | tf_op jit(solution)/shard_map/ppermute | solution.py:13
  78.7 3.2 %collective-permute-start.18 = (f32[24,256]{1,0:T(8,128)S(1)}, f32[24,256]{1,0:T(8,128)S(1)}, u32[]{:S(2)}, u32[]{:S(2)}) collective-permute-start(f32[24,256]{1,0:T(8,128)S(1)} %slice.104), channel_id=1, source_target_pairs={{0,8},{1,9},{2,10},{3,11},{4,12},{5,13},{6,14},{7,15},{8,0},{9,1},... | collective-permute-start | bytes 73736 | tf_op jit(solution)/shard_map/ppermute | solution.py:13
  81.9 1.8 %collective-permute-done.18 = f32[24,256]{1,0:T(8,128)S(1)} collective-permute-done((f32[24,256]{1,0:T(8,128)S(1)}, f32[24,256]{1,0:T(8,128)S(1)}, u32[]{:S(2)}, u32[]{:S(2)}) %collective-permute-start.18) | collective-permute-done | bytes 24608 | tf_op jit(solution)/shard_map/ppermute | solution.py:13
  84.1 1.2 %collective-permute-done.19 = f32[12,16]{0,1:T(8,128)S(1)} collective-permute-done((f32[12,16]{0,1:T(8,128)S(1)}, f32[12,16]{0,1:T(8,128)S(1)}, u32[]{:S(2)}, u32[]{:S(2)}) %collective-permute-start.19) | collective-permute-done | bytes 800 | tf_op jit(solution)/shard_map/ppermute | solution.py:13
  85.4 0.7 copy.33
  (61 shorter events, 3.3 us)
Async XLA Ops:
  0.0 44.9 %copy-start = (bf16[1,4096,32]{1,2,0:T(8,128)(2,1)S(1)}, bf16[1,4096,32]{1,2,0:T(8,128)(2,1)}, u32[]{:S(2)}) copy-start(bf16[1,4096,32]{1,2,0:T(8,128)(2,1)} %param.10) | copy-start | bytes 786436
  0.0 35.5 %copy-start.1 = (bf16[1,14336,32]{1,2,0:T(8,128)(2,1)S(1)}, bf16[1,14336,32]{1,2,0:T(8,128)(2,1)}, u32[]{:S(2)}) copy-start(bf16[1,14336,32]{1,2,0:T(8,128)(2,1)} %param.11) | copy-start | bytes 2752516
  1.0 1.5 %collective-permute-start = (bf16[12,2048]{1,0:T(8,128)(2,1)S(1)}, bf16[12,2048]{1,0:T(8,128)(2,1)S(1)}, u32[]{:S(2)}, u32[]{:S(2)}) collective-permute-start(bf16[12,2048]{1,0:T(8,128)(2,1)S(1)} %get-tuple-element.11), channel_id=1, source_target_pairs={{0,1},{1,0},{2,3},{3,2},{4,5},{5,4},{6,7},{7,6},{8,9},{9,8},{10,11... | collective-permute-start | bytes 147464 | tf_op jit(solution)/shard_map/ppermute | solution.py:13
  2.4 5.9 %collective-permute-start.9 = (bf16[12,2048]{1,0:T(8,128)(2,1)S(1)}, bf16[12,2048]{1,0:T(8,128)(2,1)S(1)}, u32[]{:S(2)}, u32[]{:S(2)}) collective-permute-start(bf16[12,2048]{1,0:T(8,128)(2,1)S(1)} %get-tuple-element.13), channel_id=1, source_target_pairs={{0,1},{1,0},{2,3},{3,2},{4,5},{5,4},{6,7},{7,6},{8,9},{9,8},{10,11... | collective-permute-start | bytes 147464 | tf_op jit(solution)/shard_map/ppermute | solution.py:13
  2.6 10.2 %collective-permute-start.1 = (bf16[24,2048]{1,0:T(8,128)(2,1)S(1)}, bf16[24,2048]{1,0:T(8,128)(2,1)S(1)}, u32[]{:S(2)}, u32[]{:S(2)}) collective-permute-start(bf16[24,2048]{1,0:T(8,128)(2,1)S(1)} %get-tuple-element.6), channel_id=1, source_target_pairs={{0,8},{1,9},{2,10},{3,11},{4,12},{5,13},{6,14},{7,15},{8,0},{9,1},... | collective-permute-start | bytes 294920 | tf_op jit(solution)/shard_map/ppermute | solution.py:13
  6.7 12.3 %collective-permute-start.2 = (bf16[24,2048]{1,0:T(8,128)(2,1)S(1)}, bf16[24,2048]{1,0:T(8,128)(2,1)S(1)}, u32[]{:S(2)}, u32[]{:S(2)}) collective-permute-start(bf16[24,2048]{1,0:T(8,128)(2,1)S(1)} %get-tuple-element.6), channel_id=1, source_target_pairs={{0,4},{1,5},{2,6},{3,7},{4,0},{5,1},{6,2},{7,3},{8,12},{9,13},{10,... | collective-permute-start | bytes 294920 | tf_op jit(solution)/shard_map/ppermute | solution.py:13
  8.3 10.7 %collective-permute-start.3 = (bf16[24,2048]{1,0:T(8,128)(2,1)S(1)}, bf16[24,2048]{1,0:T(8,128)(2,1)S(1)}, u32[]{:S(2)}, u32[]{:S(2)}) collective-permute-start(bf16[24,2048]{1,0:T(8,128)(2,1)S(1)} %get-tuple-element.6), channel_id=1, source_target_pairs={{0,12},{1,13},{2,14},{3,15},{4,8},{5,9},{6,10},{7,11},{8,4},{9,5},... | collective-permute-start | bytes 294920 | tf_op jit(solution)/shard_map/ppermute | solution.py:13
  8.3 14.6 %collective-permute-start.10 = (bf16[24,2048]{1,0:T(8,128)(2,1)S(1)}, bf16[24,2048]{1,0:T(8,128)(2,1)S(1)}, u32[]{:S(2)}, u32[]{:S(2)}) collective-permute-start(bf16[24,2048]{1,0:T(8,128)(2,1)S(1)} %get-tuple-element.8), channel_id=1, source_target_pairs={{0,8},{1,9},{2,10},{3,11},{4,12},{5,13},{6,14},{7,15},{8,0},{9,1},... | collective-permute-start | bytes 294920 | tf_op jit(solution)/shard_map/ppermute | solution.py:13
  10.3 12.6 %collective-permute-start.11 = (bf16[24,2048]{1,0:T(8,128)(2,1)S(1)}, bf16[24,2048]{1,0:T(8,128)(2,1)S(1)}, u32[]{:S(2)}, u32[]{:S(2)}) collective-permute-start(bf16[24,2048]{1,0:T(8,128)(2,1)S(1)} %get-tuple-element.8), channel_id=1, source_target_pairs={{0,4},{1,5},{2,6},{3,7},{4,0},{5,1},{6,2},{7,3},{8,12},{9,13},{10,... | collective-permute-start | bytes 294920 | tf_op jit(solution)/shard_map/ppermute | solution.py:13
  12.8 10.2 %collective-permute-start.12 = (bf16[24,2048]{1,0:T(8,128)(2,1)S(1)}, bf16[24,2048]{1,0:T(8,128)(2,1)S(1)}, u32[]{:S(2)}, u32[]{:S(2)}) collective-permute-start(bf16[24,2048]{1,0:T(8,128)(2,1)S(1)} %get-tuple-element.8), channel_id=1, source_target_pairs={{0,12},{1,13},{2,14},{3,15},{4,8},{5,9},{6,10},{7,11},{8,4},{9,5},... | collective-permute-start | bytes 294920 | tf_op jit(solution)/shard_map/ppermute | solution.py:13
  19.0 10.8 %collective-permute-start.4 = (bf16[96,2048]{1,0:T(8,128)(2,1)S(1)}, bf16[96,2048]{1,0:T(8,128)(2,1)S(1)}, u32[]{:S(2)}, u32[]{:S(2)}) collective-permute-start(bf16[96,2048]{1,0:T(8,128)(2,1)S(1)} %pad_maximum_fusion), channel_id=1, source_target_pairs={{0,2},{1,3},{2,0},{3,1},{4,6},{5,7},{6,4},{7,5},{8,10},{9,11},{10,... | collective-permute-start | bytes 1179656 | tf_op jit(solution)/shard_map/ppermute | solution.py:13
  23.0 12.4 %collective-permute-start.13 = (bf16[96,2048]{1,0:T(8,128)(2,1)S(1)}, bf16[96,2048]{1,0:T(8,128)(2,1)S(1)}, u32[]{:S(2)}, u32[]{:S(2)}) collective-permute-start(bf16[96,2048]{1,0:T(8,128)(2,1)S(1)} %pad_maximum_fusion.1), channel_id=1, source_target_pairs={{0,2},{1,3},{2,0},{3,1},{4,6},{5,7},{6,4},{7,5},{8,10},{9,11},{10,... | collective-permute-start | bytes 1179656 | tf_op jit(solution)/shard_map/ppermute | solution.py:13
  29.8 15.1 %collective-permute-start.5 = (bf16[192,2048]{1,0:T(8,128)(2,1)S(1)}, bf16[192,2048]{1,0:T(8,128)(2,1)}, u32[]{:S(2)}, u32[]{:S(2)}) collective-permute-start(bf16[192,2048]{1,0:T(8,128)(2,1)S(1)} %constant_dynamic-update-slice_fusion), channel_id=1, source_target_pairs={{0,1},{1,0},{2,3},{3,2},{4,5},{5,4},{6,7},{7,6},{8,9},{9,8},{10,11... | collective-permute-start | bytes 2359304 | tf_op jit(solution)/shard_map/ppermute | solution.py:13
  35.4 13.5 %collective-permute-start.14 = (bf16[192,2048]{1,0:T(8,128)(2,1)S(1)}, bf16[192,2048]{1,0:T(8,128)(2,1)S(1)}, u32[]{:S(2)}, u32[]{:S(2)}) collective-permute-start(bf16[192,2048]{1,0:T(8,128)(2,1)S(1)} %constant_dynamic-update-slice_fusion.5), channel_id=1, source_target_pairs={{0,1},{1,0},{2,3},{3,2},{4,5},{5,4},{6,7},{7,6},{8,9},{9,8},{10,11... | collective-permute-start | bytes 2359304 | tf_op jit(solution)/shard_map/ppermute | solution.py:13
  36.7 29.2 %all-to-all-start = ((bf16[16,32,896]{2,1,0:T(8,128)(2,1)}), bf16[16,32,896]{2,1,0:T(8,128)(2,1)S(1)}, u32[]{:S(2)}, u32[]{:S(2)}) async-start(bf16[16,32,896]{2,1,0:T(8,128)(2,1)} %copy.32), calls=%async_computation | async-start | bytes 1835008 | tf_op jit(solution)/shard_map/all_to_all | solution.py:49
  47.0 9.1 %slice-start = ((s8[7340032]{0:T(1024)(128)(4,1)}), s8[4194304]{0:T(1024)(128)(4,1)S(1)}, s32[]{:S(2)}) async-start(s8[7340032]{0:T(1024)(128)(4,1)} %bitcast.26), calls=%async_computation.1 | async-start | bytes 8388608
  47.0 9.1 %slice-start.1 = ((s8[7340032]{0:T(1024)(128)(4,1)}), s8[3145728]{0:T(1024)(128)(4,1)S(1)}, s32[]{:S(2)}) async-start(s8[7340032]{0:T(1024)(128)(4,1)} %bitcast.26), calls=%async_computation.2 | async-start | bytes 6291456
  47.0 7.1 %collective-permute-start.6 = (f32[96,32]{0,1:T(8,128)S(1)}, f32[96,32]{0,1:T(8,128)S(1)}, u32[]{:S(2)}, u32[]{:S(2)}) collective-permute-start(f32[96,32]{0,1:T(8,128)S(1)} %get-tuple-element.18), channel_id=1, source_target_pairs={{0,2},{1,3},{2,0},{3,1},{4,6},{5,7},{6,4},{7,5},{8,10},{9,11},{10,... | collective-permute-start | bytes 36872 | tf_op jit(solution)/shard_map/ppermute | solution.py:13
  54.2 7.3 %collective-permute-start.7 = (f32[48,64]{0,1:T(8,128)S(1)}, f32[48,64]{0,1:T(8,128)S(1)}, u32[]{:S(2)}, u32[]{:S(2)}) collective-permute-start(f32[48,64]{0,1:T(8,128)S(1)} %get-tuple-element.16), channel_id=1, source_target_pairs={{0,4},{1,5},{2,6},{3,7},{4,0},{5,1},{6,2},{7,3},{8,12},{9,13},{10,... | collective-permute-start | bytes 36872 | tf_op jit(solution)/shard_map/ppermute | solution.py:13
  66.7 1.5 %collective-permute-start.15 = (f32[192,256]{1,0:T(8,128)S(1)}, f32[192,256]{1,0:T(8,128)S(1)}, u32[]{:S(2)}, u32[]{:S(2)}) collective-permute-start(f32[192,256]{1,0:T(8,128)S(1)} %convolution_add_fusion), channel_id=1, source_target_pairs={{0,1},{1,0},{2,3},{3,2},{4,5},{5,4},{6,7},{7,6},{8,9},{9,8},{10,11... | collective-permute-start | bytes 589832 | tf_op jit(solution)/shard_map/ppermute | solution.py:13
  68.5 5.0 %collective-permute-start.16 = (f32[96,256]{1,0:T(8,128)S(1)}, f32[96,256]{1,0:T(8,128)S(1)}, u32[]{:S(2)}, u32[]{:S(2)}) collective-permute-start(f32[96,256]{1,0:T(8,128)S(1)} %slice.100), channel_id=1, source_target_pairs={{0,2},{1,3},{2,0},{3,1},{4,6},{5,7},{6,4},{7,5},{8,10},{9,11},{10,... | collective-permute-start | bytes 294920 | tf_op jit(solution)/shard_map/ppermute | solution.py:13
  73.6 5.1 %collective-permute-start.17 = (f32[48,256]{1,0:T(8,128)S(1)}, f32[48,256]{1,0:T(8,128)S(1)}, u32[]{:S(2)}, u32[]{:S(2)}) collective-permute-start(f32[48,256]{1,0:T(8,128)S(1)} %slice.102), channel_id=1, source_target_pairs={{0,4},{1,5},{2,6},{3,7},{4,0},{5,1},{6,2},{7,3},{8,12},{9,13},{10,... | collective-permute-start | bytes 147464 | tf_op jit(solution)/shard_map/ppermute | solution.py:13
  76.6 5.3 %collective-permute-start.8 = (f32[24,128]{1,0:T(8,128)S(1)}, f32[24,128]{1,0:T(8,128)S(1)}, u32[]{:S(2)}, u32[]{:S(2)}) collective-permute-start(f32[24,128]{1,0:T(8,128)S(1)} %get-tuple-element.20), channel_id=1, source_target_pairs={{0,8},{1,9},{2,10},{3,11},{4,12},{5,13},{6,14},{7,15},{8,0},{9,1},... | collective-permute-start | bytes 36872 | tf_op jit(solution)/shard_map/ppermute | solution.py:13
  78.7 5.0 %collective-permute-start.18 = (f32[24,256]{1,0:T(8,128)S(1)}, f32[24,256]{1,0:T(8,128)S(1)}, u32[]{:S(2)}, u32[]{:S(2)}) collective-permute-start(f32[24,256]{1,0:T(8,128)S(1)} %slice.104), channel_id=1, source_target_pairs={{0,8},{1,9},{2,10},{3,11},{4,12},{5,13},{6,14},{7,15},{8,0},{9,1},... | collective-permute-start | bytes 73736 | tf_op jit(solution)/shard_map/ppermute | solution.py:13
  84.1 1.2 %collective-permute-start.19 = (f32[12,16]{0,1:T(8,128)S(1)}, f32[12,16]{0,1:T(8,128)S(1)}, u32[]{:S(2)}, u32[]{:S(2)}) collective-permute-start(f32[12,16]{0,1:T(8,128)S(1)} %slice_select_fusion), channel_id=1, source_target_pairs={{0,1},{1,0},{2,3},{3,2},{4,5},{5,4},{6,7},{7,6},{8,9},{9,8},{10,11... | collective-permute-start | bytes 2312 | tf_op jit(solution)/shard_map/ppermute | solution.py:13
where the time goes:
time: 86.3 us; the launch traced here: 86 us
  starting transfers between devices  41.8 us (48%)
  waiting for transfers between devices  28.6 us (33%)
  matrix products  10.7 us (12%)
  other arithmetic  2.38 us (3%)
  local copies, waits for them, and re-layouts  2.3 us (3%)
    ppermute x20, starting transfers between devices, swap(): return lax.ppermute(x, AXIS, [(i, i ^ bit) for i in range(n)])  33.7 us
    ppermute x20, waiting for transfers between devices, swap(): return lax.ppermute(x, AXIS, [(i, i ^ bit) for i in range(n)])  24.2 us
    all_to_all x1, starting transfers between devices, body(): lax.all_to_all(blocks, AXIS, split_axis=0, concat_axis=0, tiled=True)  8.12 us
    dot_general x1, matrix products, body(): gate = jnp.dot(whole, gate_weight, preferred_element_type=F32)  5.16 us
    all_to_all x1, waiting for transfers between devices, body(): lax.all_to_all(blocks, AXIS, split_axis=0, concat_axis=0, tiled=True)  4.41 us
    select_n x6, other arithmetic, pick(): return jnp.where(flag == 0, when_zero, when_one)  2.12 us
    dot_general x1, matrix products, body(): left = jnp.dot(grads, query_left[0], preferred_element_type=F32)  1.97 us
    dot_general x1, matrix products, body(): up = jnp.dot(whole, up_weight, preferred_element_type=F32)  1.87 us
  transfers between devices with their start and end apart: 21, of which 10 were waited for; matrix products, arithmetic and copies ran while one was open for 14% of the time, Pallas kernels for 0%

commit v1 on v0

--- a/solution.py
+++ b/solution.py
@@ -6,6 +6,22 @@
 AXIS = "query"
 F32 = jnp.float32
 BF16 = jnp.bfloat16
+
+
+def pairwise_exchange(x, axis, split, join):
+    ways, here = (lax.axis_size(axis), lax.axis_index(axis))
+    width = x.shape[split] // ways
+    lengths = list(x.shape)
+    lengths[split] = width
+    height = lengths[join]
+    lengths[join] = height * ways
+    full = jnp.zeros(lengths, x.dtype)
+    for mask in range(ways):
+        part = lax.dynamic_slice_in_dim(x, (here ^ mask) * width, width, axis=split)
+        if mask:
+            part = lax.ppermute(part, axis, [(d, d ^ mask) for d in range(ways)])
+        full = lax.dynamic_update_slice_in_dim(full, part, (here ^ mask) * height, axis=join)
+    return full
 
 
 def swap(x, bit):
@@ -46,7 +62,7 @@
     rank = query_right.shape[2]
     cols = gate_weight.shape[1]
     blocks = query_right[0].T.reshape(rank, n, cols).transpose(1, 0, 2)
-    factors = lax.all_to_all(blocks, AXIS, split_axis=0, concat_axis=0, tiled=True)
+    factors = pairwise_exchange(blocks, AXIS, 0, 0)
     factors = factors.reshape(n // 2, 2, rank, cols)
     keep_factors = pick(core, factors[:, 0], factors[:, 1]).reshape(n // 2 * rank, cols)
     send_factors = pick(core, factors[:, 1], factors[:, 0]).reshape(n // 2 * rank, cols)

time: 86.3 us -> 100 us (1.16)
  waiting for transfers between devices: 28.6 us -> 37 us
  starting transfers between devices: 41.8 us -> 49.7 us
  matrix products: 10.7 us -> 5.99 us
  local copies, waits for them, and re-layouts: 2.3 us -> 6.2 us
  other arithmetic: 2.38 us -> 0.55 us
    ppermute x0 -> x15, starting transfers between devices: none -> 26.8 us  [pairwise_exchange(): part = lax.ppermute(part, axis, [(d, d ^ mask) for d in range(ways)])]
    ppermute x20, waiting for transfers between devices: 24.2 us -> 36.7 us  [swap(): return lax.ppermute(x, AXIS, [(i, i ^ bit) for i in range(n)])]
    ppermute x20, starting transfers between devices: 33.7 us -> 22.8 us  [swap(): return lax.ppermute(x, AXIS, [(i, i ^ bit) for i in range(n)])]
    all_to_all x1 -> x0, starting transfers between devices: 8.12 us -> none  [body(): lax.all_to_all(blocks, AXIS, split_axis=0, concat_axis=0, tiled=True)]
    all_to_all x1 -> x0, waiting for transfers between devices: 4.41 us -> none  [body(): lax.all_to_all(blocks, AXIS, split_axis=0, concat_axis=0, tiled=True)]
    dot_general x1, matrix products: 5.16 us -> 1.86 us  [body(): gate = jnp.dot(whole, gate_weight, preferred_element_type=F32)]
    another operation x0 -> x1, local copies, waits for them, and re-layouts: none -> 2.67 us
    unnamed x15 -> x36, local copies, waits for them, and re-layouts: 0.16 us -> 2.18 us
  transfers between devices with their start and end apart: 21 -> 35, of which waited for: 10 -> 13; matrix products, arithmetic and copies ran while one was open for 14% -> 7% of each run, Pallas kernels for 0% -> 0%
where the time goes in v1:
time: 100 us
  starting transfers between devices  49.7 us (50%)
  waiting for transfers between devices  37 us (37%)
  local copies, waits for them, and re-layouts  6.2 us (6%)
  matrix products  5.99 us (6%)
    ppermute x20, waiting for transfers between devices, swap(): return lax.ppermute(x, AXIS, [(i, i ^ bit) for i in range(n)])  36.7 us
    ppermute x15, starting transfers between devices, pairwise_exchange(): part = lax.ppermute(part, axis, [(d, d ^ mask) for d in range(ways)])  26.8 us
    ppermute x20, starting transfers between devices, swap(): return lax.ppermute(x, AXIS, [(i, i ^ bit) for i in range(n)])  22.8 us
    another operation x1, local copies, waits for them, and re-layouts  2.67 us
    unnamed x36, local copies, waits for them, and re-layouts  2.18 us
  transfers between devices with their start and end apart: 35, of which 13 were waited for; matrix products, arithmetic and copies ran while one was open for 7% of the time, Pallas kernels for 0%

profile of v1, /device:TPU:0, one launch (start us, length us, event | category | flops | bytes accessed | tf_op | source)
XLA Modules:
  0.0 100.1 jit_solution(17699926253830695859)
XLA Ops:
  0.0 1.3 %copy.43 = bf16[4,8,16,896]{3,2,1,0:T(8,128)(2,1)S(1)} copy(bf16[4,8,16,896]{3,1,2,0:T(8,128)(2,1)} %bitcast.70) | data formatting | bytes 1835008
  1.4 2.7 %constant_dynamic-slice_fusion = (bf16[32,1,896]{2,1,0:T(2,128)(2,1)S(1)}, bf16[32,1,896]{2,1,0:T(2,128)(2,1)S(1)}, bf16[32,1,896]{2,1,0:T(2,128)(2,1)S(1)}, bf1...) fusion(bf16[32,16,896]{2,1,0:T(8,128)(2,1)S(1)} %bitcast.64, ...), kind=kLoop, calls=%fused_computation.79 | loop fusion | bytes 1835072 | tf_op jit(solution)/shard_map/dynamic-slice.15
  5.2 2.6 %collective-permute-start.16 = (bf16[1,32,896]{2,1,0:T(8,128)(2,1)S(1)}, bf16[1,32,896]{2,1,0:T(8,128)(2,1)S(1)}, u32[]{:S(2)}, u32[]{:S(2)}) collective-permute-start(bf16[1,32,896]{2,1,0:T(8,128)(2,1)S(1)} %bitcast.82), channel_id=1, source_target_pairs={{0,2},{1,3},{2,0},{3,1},{4,6},{5,7},{6,4},{7,5},{8,10},{9,11},{10,... | collective-permute-start | bytes 172040 | tf_op jit(solution)/shard_map/ppermute | solution.py:22
  8.0 1.8 %collective-permute-start.18 = (bf16[1,32,896]{2,1,0:T(8,128)(2,1)S(1)}, bf16[1,32,896]{2,1,0:T(8,128)(2,1)S(1)}, u32[]{:S(2)}, u32[]{:S(2)}) collective-permute-start(bf16[1,32,896]{2,1,0:T(8,128)(2,1)S(1)} %bitcast.79), channel_id=1, source_target_pairs={{0,4},{1,5},{2,6},{3,7},{4,0},{5,1},{6,2},{7,3},{8,12},{9,13},{10,... | collective-permute-start | bytes 172040 | tf_op jit(solution)/shard_map/ppermute | solution.py:22
  11.4 1.0 %collective-permute-done = bf16[12,2048]{1,0:T(8,128)(2,1)S(1)} collective-permute-done((bf16[12,2048]{1,0:T(8,128)(2,1)S(1)}, bf16[12,2048]{1,0:T(8,128)(2,1)S(1)}, u32[]{:S(2)}, u32[]{:S(2)}) %collective-permute-start) | collective-permute-done | bytes 49184 | tf_op jit(solution)/shard_map/ppermute | solution.py:29
  12.5 2.8 %collective-permute-start.20 = (bf16[1,32,896]{2,1,0:T(8,128)(2,1)S(1)}, bf16[1,32,896]{2,1,0:T(8,128)(2,1)S(1)}, u32[]{:S(2)}, u32[]{:S(2)}) collective-permute-start(bf16[1,32,896]{2,1,0:T(8,128)(2,1)S(1)} %bitcast.83), channel_id=1, source_target_pairs={{0,6},{1,7},{2,4},{3,5},{4,2},{5,3},{6,0},{7,1},{8,14},{9,15},{10,... | collective-permute-start | bytes 172040 | tf_op jit(solution)/shard_map/ppermute | solution.py:22
  15.5 2.7 %collective-permute-start.22 = (bf16[1,32,896]{2,1,0:T(8,128)(2,1)S(1)}, bf16[1,32,896]{2,1,0:T(8,128)(2,1)S(1)}, u32[]{:S(2)}, u32[]{:S(2)}) collective-permute-start(bf16[1,32,896]{2,1,0:T(8,128)(2,1)S(1)} %bitcast.78), channel_id=1, source_target_pairs={{0,8},{1,9},{2,10},{3,11},{4,12},{5,13},{6,14},{7,15},{8,0},{9,1},... | collective-permute-start | bytes 172040 | tf_op jit(solution)/shard_map/ppermute | solution.py:22
  18.3 3.6 %collective-permute-start.24 = (bf16[1,32,896]{2,1,0:T(8,128)(2,1)S(1)}, bf16[1,32,896]{2,1,0:T(8,128)(2,1)S(1)}, u32[]{:S(2)}, u32[]{:S(2)}) collective-permute-start(bf16[1,32,896]{2,1,0:T(8,128)(2,1)S(1)} %bitcast.76), channel_id=1, source_target_pairs={{0,10},{1,11},{2,8},{3,9},{4,14},{5,15},{6,12},{7,13},{8,2},{9,3},... | collective-permute-start | bytes 172040 | tf_op jit(solution)/shard_map/ppermute | solution.py:22
  22.1 3.6 %collective-permute-start.26 = (bf16[1,32,896]{2,1,0:T(8,128)(2,1)S(1)}, bf16[1,32,896]{2,1,0:T(8,128)(2,1)S(1)}, u32[]{:S(2)}, u32[]{:S(2)}) collective-permute-start(bf16[1,32,896]{2,1,0:T(8,128)(2,1)S(1)} %bitcast.74), channel_id=1, source_target_pairs={{0,12},{1,13},{2,14},{3,15},{4,8},{5,9},{6,10},{7,11},{8,4},{9,5},... | collective-permute-start | bytes 172040 | tf_op jit(solution)/shard_map/ppermute | solution.py:22
  26.5 4.8 %collective-permute-start.28 = (bf16[1,32,896]{2,1,0:T(8,128)(2,1)S(1)}, bf16[1,32,896]{2,1,0:T(8,128)(2,1)S(1)}, u32[]{:S(2)}, u32[]{:S(2)}) collective-permute-start(bf16[1,32,896]{2,1,0:T(8,128)(2,1)S(1)} %bitcast.72), channel_id=1, source_target_pairs={{0,14},{1,15},{2,12},{3,13},{4,10},{5,11},{6,8},{7,9},{8,6},{9,7},... | collective-permute-start | bytes 172040 | tf_op jit(solution)/shard_map/ppermute | solution.py:22
  31.3 3.3 %collective-permute-start.29 = (bf16[1,32,896]{2,1,0:T(8,128)(2,1)S(1)}, bf16[1,32,896]{2,1,0:T(8,128)(2,1)S(1)}, u32[]{:S(2)}, u32[]{:S(2)}) collective-permute-start(bf16[1,32,896]{2,1,0:T(8,128)(2,1)S(1)} %bitcast.71), channel_id=1, source_target_pairs={{0,15},{1,14},{2,13},{3,12},{4,11},{5,10},{6,9},{7,8},{8,7},{9,6},... | collective-permute-start | bytes 172040 | tf_op jit(solution)/shard_map/ppermute | solution.py:22
  35.6 3.8 %collective-permute-start.12 = (bf16[24,2048]{1,0:T(8,128)(2,1)S(1)}, bf16[24,2048]{1,0:T(8,128)(2,1)S(1)}, u32[]{:S(2)}, u32[]{:S(2)}) collective-permute-start(bf16[24,2048]{1,0:T(8,128)(2,1)S(1)} %get-tuple-element.8), channel_id=1, source_target_pairs={{0,12},{1,13},{2,14},{3,15},{4,8},{5,9},{6,10},{7,11},{8,4},{9,5},... | collective-permute-start | bytes 294920 | tf_op jit(solution)/shard_map/ppermute | solution.py:29
  39.4 4.2 %collective-permute-start.1 = (bf16[24,2048]{1,0:T(8,128)(2,1)S(1)}, bf16[24,2048]{1,0:T(8,128)(2,1)S(1)}, u32[]{:S(2)}, u32[]{:S(2)}) collective-permute-start(bf16[24,2048]{1,0:T(8,128)(2,1)S(1)} %get-tuple-element.6), channel_id=1, source_target_pairs={{0,8},{1,9},{2,10},{3,11},{4,12},{5,13},{6,14},{7,15},{8,0},{9,1},... | collective-permute-start | bytes 294920 | tf_op jit(solution)/shard_map/ppermute | solution.py:29
  43.6 4.8 %collective-permute-done.10 = bf16[24,2048]{1,0:T(8,128)(2,1)S(1)} collective-permute-done((bf16[24,2048]{1,0:T(8,128)(2,1)S(1)}, bf16[24,2048]{1,0:T(8,128)(2,1)S(1)}, u32[]{:S(2)}, u32[]{:S(2)}) %collective-permute-start.10) | collective-permute-done | bytes 98336 | tf_op jit(solution)/shard_map/ppermute | solution.py:29
  48.5 2.6 %collective-permute-start.3 = (bf16[24,2048]{1,0:T(8,128)(2,1)S(1)}, bf16[24,2048]{1,0:T(8,128)(2,1)S(1)}, u32[]{:S(2)}, u32[]{:S(2)}) collective-permute-start(bf16[24,2048]{1,0:T(8,128)(2,1)S(1)} %get-tuple-element.6), channel_id=1, source_target_pairs={{0,12},{1,13},{2,14},{3,15},{4,8},{5,9},{6,10},{7,11},{8,4},{9,5},... | collective-permute-start | bytes 294920 | tf_op jit(solution)/shard_map/ppermute | solution.py:29
  51.2 1.6 %collective-permute-start.13 = (bf16[96,2048]{1,0:T(8,128)(2,1)S(1)}, bf16[96,2048]{1,0:T(8,128)(2,1)S(1)}, u32[]{:S(2)}, u32[]{:S(2)}) collective-permute-start(bf16[96,2048]{1,0:T(8,128)(2,1)S(1)} %pad_maximum_fusion.1), channel_id=1, source_target_pairs={{0,2},{1,3},{2,0},{3,1},{4,6},{5,7},{6,4},{7,5},{8,10},{9,11},{10,... | collective-permute-start | bytes 1179656 | tf_op jit(solution)/shard_map/ppermute | solution.py:29
  52.8 4.1 %collective-permute-done.2 = bf16[24,2048]{1,0:T(8,128)(2,1)S(1)} collective-permute-done((bf16[24,2048]{1,0:T(8,128)(2,1)S(1)}, bf16[24,2048]{1,0:T(8,128)(2,1)S(1)}, u32[]{:S(2)}, u32[]{:S(2)}) %collective-permute-start.2) | collective-permute-done | bytes 98336 | tf_op jit(solution)/shard_map/ppermute | solution.py:29
  56.9 1.6 %collective-permute-start.4 = (bf16[96,2048]{1,0:T(8,128)(2,1)S(1)}, bf16[96,2048]{1,0:T(8,128)(2,1)S(1)}, u32[]{:S(2)}, u32[]{:S(2)}) collective-permute-start(bf16[96,2048]{1,0:T(8,128)(2,1)S(1)} %pad_maximum_fusion), channel_id=1, source_target_pairs={{0,2},{1,3},{2,0},{3,1},{4,6},{5,7},{6,4},{7,5},{8,10},{9,11},{10,... | collective-permute-start | bytes 1179656 | tf_op jit(solution)/shard_map/ppermute | solution.py:29
  58.6 11.8 %collective-permute-done.4 = bf16[96,2048]{1,0:T(8,128)(2,1)S(1)} collective-permute-done((bf16[96,2048]{1,0:T(8,128)(2,1)S(1)}, bf16[96,2048]{1,0:T(8,128)(2,1)S(1)}, u32[]{:S(2)}, u32[]{:S(2)}) %collective-permute-start.4) | collective-permute-done | bytes 393248 | tf_op jit(solution)/shard_map/ppermute | solution.py:29
  71.3 1.5 %collective-permute-done.5 = bf16[192,2048]{1,0:T(8,128)(2,1)S(1)} collective-permute-done((bf16[192,2048]{1,0:T(8,128)(2,1)S(1)}, bf16[192,2048]{1,0:T(8,128)(2,1)S(1)}, u32[]{:S(2)}, u32[]{:S(2)}) %collective-permute-start.5) | collective-permute-done | bytes 786464 | tf_op jit(solution)/shard_map/ppermute | solution.py:29
  73.5 1.5 %collective-permute-start.6 = (f32[96,32]{0,1:T(8,128)S(1)}, f32[96,32]{0,1:T(8,128)S(1)}, u32[]{:S(2)}, u32[]{:S(2)}) collective-permute-start(f32[96,32]{0,1:T(8,128)S(1)} %get-tuple-element.34), channel_id=1, source_target_pairs={{0,2},{1,3},{2,0},{3,1},{4,6},{5,7},{6,4},{7,5},{8,10},{9,11},{10,... | collective-permute-start | bytes 36872 | tf_op jit(solution)/shard_map/ppermute | solution.py:29
  75.1 1.9 %fusion.10 = f32[192,896]{1,0:T(8,128)S(1)} fusion(bf16[4096,896]{1,0:T(8,128)(2,1)S(1)} %bitcast.86, bf16[192,2048]{1,0:T(8,128)(2,1)S(1)} %collective-permute-done.14, bf16[192,2048]{1,0:T(8,128)(2,1)S(1)} %constant_dynamic-update-slice_fusion.5, pred[]{:T(512)S(6)} %eq.10), kind=kOutput, calls=%fused_computation.21 | convolution fusion | flops 1416364032 | bytes 9601025 | tf_op jit(solution)/shard_map/dot_general | solution.py:71
  77.0 1.9 %multiply_multiply_fusion = f32[192,896]{1,0:T(8,128)S(1)} fusion(f32[192,896]{1,0:T(8,128)S(1)} %fusion.10, bf16[4096,896]{1,0:T(8,128)(2,1)S(1)} %bitcast.88, bf16[192,2048]{1,0:T(8,128)(2,1)S(1)} %collective-permute-done.14, bf16[192,2048]{1,0:T(8,128)(2,1)S(1)} %constant_dynamic-update-slice_fusion.5, pred[]{:T(512)S(6)} %eq.10), kind=kOutput, calls=%fused_computation.15 | convolution fusion | flops 1417224192 | bytes 10289153 | tf_op jit(solution)/shard_map/dot_general | solution.py:72
  80.9 2.7 %collective-permute-done.7 = f32[48,64]{0,1:T(8,128)S(1)} collective-permute-done((f32[48,64]{0,1:T(8,128)S(1)}, f32[48,64]{0,1:T(8,128)S(1)}, u32[]{:S(2)}, u32[]{:S(2)}) %collective-permute-start.7) | collective-permute-done | bytes 12320 | tf_op jit(solution)/shard_map/ppermute | solution.py:29
  84.0 1.4 %collective-permute-start.31 = (f32[96,256]{1,0:T(8,128)S(1)}, f32[96,256]{1,0:T(8,128)S(1)}, u32[]{:S(2)}, u32[]{:S(2)}) collective-permute-start(f32[96,256]{1,0:T(8,128)S(1)} %slice.100), channel_id=1, source_target_pairs={{0,2},{1,3},{2,0},{3,1},{4,6},{5,7},{6,4},{7,5},{8,10},{9,11},{10,... | collective-permute-start | bytes 294920 | tf_op jit(solution)/shard_map/ppermute | solution.py:29
  85.5 3.2 %collective-permute-done.31 = f32[96,256]{1,0:T(8,128)S(1)} collective-permute-done((f32[96,256]{1,0:T(8,128)S(1)}, f32[96,256]{1,0:T(8,128)S(1)}, u32[]{:S(2)}, u32[]{:S(2)}) %collective-permute-start.31) | collective-permute-done | bytes 98336 | tf_op jit(solution)/shard_map/ppermute | solution.py:29
  88.7 0.9 collective-permute-start.32
  89.6 0.9 collective-permute-start.8
  90.6 2.3 %collective-permute-done.32 = f32[48,256]{1,0:T(8,128)S(1)} collective-permute-done((f32[48,256]{1,0:T(8,128)S(1)}, f32[48,256]{1,0:T(8,128)S(1)}, u32[]{:S(2)}, u32[]{:S(2)}) %collective-permute-start.32) | collective-permute-done | bytes 49184 | tf_op jit(solution)/shard_map/ppermute | solution.py:29
  92.9 1.7 %collective-permute-start.33 = (f32[24,256]{1,0:T(8,128)S(1)}, f32[24,256]{1,0:T(8,128)S(1)}, u32[]{:S(2)}, u32[]{:S(2)}) collective-permute-start(f32[24,256]{1,0:T(8,128)S(1)} %slice.104), channel_id=1, source_target_pairs={{0,8},{1,9},{2,10},{3,11},{4,12},{5,13},{6,14},{7,15},{8,0},{9,1},... | collective-permute-start | bytes 73736 | tf_op jit(solution)/shard_map/ppermute | solution.py:29
  94.6 3.1 %collective-permute-done.33 = f32[24,256]{1,0:T(8,128)S(1)} collective-permute-done((f32[24,256]{1,0:T(8,128)S(1)}, f32[24,256]{1,0:T(8,128)S(1)}, u32[]{:S(2)}, u32[]{:S(2)}) %collective-permute-start.33) | collective-permute-done | bytes 24608 | tf_op jit(solution)/shard_map/ppermute | solution.py:29
  98.2 1.2 %collective-permute-done.34 = f32[12,16]{0,1:T(8,128)S(1)} collective-permute-done((f32[12,16]{0,1:T(8,128)S(1)}, f32[12,16]{0,1:T(8,128)S(1)}, u32[]{:S(2)}, u32[]{:S(2)}) %collective-permute-start.34) | collective-permute-done | bytes 800 | tf_op jit(solution)/shard_map/ppermute | solution.py:29
  (128 shorter events, 10.4 us)
Async XLA Ops:
  4.7 7.8 %collective-permute-start.15 = (bf16[1,32,896]{2,1,0:T(8,128)(2,1)}, bf16[1,32,896]{2,1,0:T(8,128)(2,1)S(1)}, u32[]{:S(2)}, u32[]{:S(2)}) collective-permute-start(bf16[1,32,896]{2,1,0:T(8,128)(2,1)} %bitcast.63), channel_id=1, source_target_pairs={{0,1},{1,0},{2,3},{3,2},{4,5},{5,4},{6,7},{7,6},{8,9},{9,8},{10,11... | collective-permute-start | bytes 172040 | tf_op jit(solution)/shard_map/ppermute | solution.py:22
  5.2 10.1 %collective-permute-start.16 = (bf16[1,32,896]{2,1,0:T(8,128)(2,1)S(1)}, bf16[1,32,896]{2,1,0:T(8,128)(2,1)S(1)}, u32[]{:S(2)}, u32[]{:S(2)}) collective-permute-start(bf16[1,32,896]{2,1,0:T(8,128)(2,1)S(1)} %bitcast.82), channel_id=1, source_target_pairs={{0,2},{1,3},{2,0},{3,1},{4,6},{5,7},{6,4},{7,5},{8,10},{9,11},{10,... | collective-permute-start | bytes 172040 | tf_op jit(solution)/shard_map/ppermute | solution.py:22
  7.8 7.7 %collective-permute-start.17 = (bf16[1,32,896]{2,1,0:T(8,128)(2,1)S(1)}, bf16[1,32,896]{2,1,0:T(8,128)(2,1)S(1)}, u32[]{:S(2)}, u32[]{:S(2)}) collective-permute-start(bf16[1,32,896]{2,1,0:T(8,128)(2,1)S(1)} %bitcast.81), channel_id=1, source_target_pairs={{0,3},{1,2},{2,1},{3,0},{4,7},{5,6},{6,5},{7,4},{8,11},{9,10},{10,... | collective-permute-start | bytes 172040 | tf_op jit(solution)/shard_map/ppermute | solution.py:22
  8.0 10.2 %collective-permute-start.18 = (bf16[1,32,896]{2,1,0:T(8,128)(2,1)S(1)}, bf16[1,32,896]{2,1,0:T(8,128)(2,1)S(1)}, u32[]{:S(2)}, u32[]{:S(2)}) collective-permute-start(bf16[1,32,896]{2,1,0:T(8,128)(2,1)S(1)} %bitcast.79), channel_id=1, source_target_pairs={{0,4},{1,5},{2,6},{3,7},{4,0},{5,1},{6,2},{7,3},{8,12},{9,13},{10,... | collective-permute-start | bytes 172040 | tf_op jit(solution)/shard_map/ppermute | solution.py:22
  12.5 5.9 %collective-permute-start.19 = (bf16[1,32,896]{2,1,0:T(8,128)(2,1)S(1)}, bf16[1,32,896]{2,1,0:T(8,128)(2,1)S(1)}, u32[]{:S(2)}, u32[]{:S(2)}) collective-permute-start(bf16[1,32,896]{2,1,0:T(8,128)(2,1)S(1)} %bitcast.84), channel_id=1, source_target_pairs={{0,5},{1,4},{2,7},{3,6},{4,1},{5,0},{6,3},{7,2},{8,13},{9,12},{10,... | collective-permute-start | bytes 172040 | tf_op jit(solution)/shard_map/ppermute | solution.py:22
  12.5 9.5 %collective-permute-start.20 = (bf16[1,32,896]{2,1,0:T(8,128)(2,1)S(1)}, bf16[1,32,896]{2,1,0:T(8,128)(2,1)S(1)}, u32[]{:S(2)}, u32[]{:S(2)}) collective-permute-start(bf16[1,32,896]{2,1,0:T(8,128)(2,1)S(1)} %bitcast.83), channel_id=1, source_target_pairs={{0,6},{1,7},{2,4},{3,5},{4,2},{5,3},{6,0},{7,1},{8,14},{9,15},{10,... | collective-permute-start | bytes 172040 | tf_op jit(solution)/shard_map/ppermute | solution.py:22
  15.4 6.8 %collective-permute-start.21 = (bf16[1,32,896]{2,1,0:T(8,128)(2,1)S(1)}, bf16[1,32,896]{2,1,0:T(8,128)(2,1)S(1)}, u32[]{:S(2)}, u32[]{:S(2)}) collective-permute-start(bf16[1,32,896]{2,1,0:T(8,128)(2,1)S(1)} %bitcast.80), channel_id=1, source_target_pairs={{0,7},{1,6},{2,5},{3,4},{4,3},{5,2},{6,1},{7,0},{8,15},{9,14},{10,... | collective-permute-start | bytes 172040 | tf_op jit(solution)/shard_map/ppermute | solution.py:22
  15.5 10.3 %collective-permute-start.22 = (bf16[1,32,896]{2,1,0:T(8,128)(2,1)S(1)}, bf16[1,32,896]{2,1,0:T(8,128)(2,1)S(1)}, u32[]{:S(2)}, u32[]{:S(2)}) collective-permute-start(bf16[1,32,896]{2,1,0:T(8,128)(2,1)S(1)} %bitcast.78), channel_id=1, source_target_pairs={{0,8},{1,9},{2,10},{3,11},{4,12},{5,13},{6,14},{7,15},{8,0},{9,1},... | collective-permute-start | bytes 172040 | tf_op jit(solution)/shard_map/ppermute | solution.py:22
  18.2 8.3 %collective-permute-start.23 = (bf16[1,32,896]{2,1,0:T(8,128)(2,1)S(1)}, bf16[1,32,896]{2,1,0:T(8,128)(2,1)S(1)}, u32[]{:S(2)}, u32[]{:S(2)}) collective-permute-start(bf16[1,32,896]{2,1,0:T(8,128)(2,1)S(1)} %bitcast.77), channel_id=1, source_target_pairs={{0,9},{1,8},{2,11},{3,10},{4,13},{5,12},{6,15},{7,14},{8,1},{9,0},... | collective-permute-start | bytes 172040 | tf_op jit(solution)/shard_map/ppermute | solution.py:22
  18.3 13.0 %collective-permute-start.24 = (bf16[1,32,896]{2,1,0:T(8,128)(2,1)S(1)}, bf16[1,32,896]{2,1,0:T(8,128)(2,1)S(1)}, u32[]{:S(2)}, u32[]{:S(2)}) collective-permute-start(bf16[1,32,896]{2,1,0:T(8,128)(2,1)S(1)} %bitcast.76), channel_id=1, source_target_pairs={{0,10},{1,11},{2,8},{3,9},{4,14},{5,15},{6,12},{7,13},{8,2},{9,3},... | collective-permute-start | bytes 172040 | tf_op jit(solution)/shard_map/ppermute | solution.py:22
  22.0 12.8 %collective-permute-start.25 = (bf16[1,32,896]{2,1,0:T(8,128)(2,1)S(1)}, bf16[1,32,896]{2,1,0:T(8,128)(2,1)S(1)}, u32[]{:S(2)}, u32[]{:S(2)}) collective-permute-start(bf16[1,32,896]{2,1,0:T(8,128)(2,1)S(1)} %bitcast.75), channel_id=1, source_target_pairs={{0,11},{1,10},{2,9},{3,8},{4,15},{5,14},{6,13},{7,12},{8,3},{9,2},... | collective-permute-start | bytes 172040 | tf_op jit(solution)/shard_map/ppermute | solution.py:22
  22.1 12.7 %collective-permute-start.26 = (bf16[1,32,896]{2,1,0:T(8,128)(2,1)S(1)}, bf16[1,32,896]{2,1,0:T(8,128)(2,1)S(1)}, u32[]{:S(2)}, u32[]{:S(2)}) collective-permute-start(bf16[1,32,896]{2,1,0:T(8,128)(2,1)S(1)} %bitcast.74), channel_id=1, source_target_pairs={{0,12},{1,13},{2,14},{3,15},{4,8},{5,9},{6,10},{7,11},{8,4},{9,5},... | collective-permute-start | bytes 172040 | tf_op jit(solution)/shard_map/ppermute | solution.py:22
  25.7 9.9 %collective-permute-start.27 = (bf16[1,32,896]{2,1,0:T(8,128)(2,1)S(1)}, bf16[1,32,896]{2,1,0:T(8,128)(2,1)S(1)}, u32[]{:S(2)}, u32[]{:S(2)}) collective-permute-start(bf16[1,32,896]{2,1,0:T(8,128)(2,1)S(1)} %bitcast.73), channel_id=1, source_target_pairs={{0,13},{1,12},{2,15},{3,14},{4,9},{5,8},{6,11},{7,10},{8,5},{9,4},... | collective-permute-start | bytes 172040 | tf_op jit(solution)/shard_map/ppermute | solution.py:22
  26.5 12.9 %collective-permute-start.28 = (bf16[1,32,896]{2,1,0:T(8,128)(2,1)S(1)}, bf16[1,32,896]{2,1,0:T(8,128)(2,1)S(1)}, u32[]{:S(2)}, u32[]{:S(2)}) collective-permute-start(bf16[1,32,896]{2,1,0:T(8,128)(2,1)S(1)} %bitcast.72), channel_id=1, source_target_pairs={{0,14},{1,15},{2,12},{3,13},{4,10},{5,11},{6,8},{7,9},{8,6},{9,7},... | collective-permute-start | bytes 172040 | tf_op jit(solution)/shard_map/ppermute | solution.py:22
  31.3 39.8 %collective-permute-start.29 = (bf16[1,32,896]{2,1,0:T(8,128)(2,1)S(1)}, bf16[1,32,896]{2,1,0:T(8,128)(2,1)S(1)}, u32[]{:S(2)}, u32[]{:S(2)}) collective-permute-start(bf16[1,32,896]{2,1,0:T(8,128)(2,1)S(1)} %bitcast.71), channel_id=1, source_target_pairs={{0,15},{1,14},{2,13},{3,12},{4,11},{5,10},{6,9},{7,8},{8,7},{9,6},... | collective-permute-start | bytes 172040 | tf_op jit(solution)/shard_map/ppermute | solution.py:22
  34.8 13.7 %collective-permute-start.10 = (bf16[24,2048]{1,0:T(8,128)(2,1)S(1)}, bf16[24,2048]{1,0:T(8,128)(2,1)S(1)}, u32[]{:S(2)}, u32[]{:S(2)}) collective-permute-start(bf16[24,2048]{1,0:T(8,128)(2,1)S(1)} %get-tuple-element.8), channel_id=1, source_target_pairs={{0,8},{1,9},{2,10},{3,11},{4,12},{5,13},{6,14},{7,15},{8,0},{9,1},... | collective-permute-start | bytes 294920 | tf_op jit(solution)/shard_map/ppermute | solution.py:29
  34.8 13.7 %collective-permute-start.11 = (bf16[24,2048]{1,0:T(8,128)(2,1)S(1)}, bf16[24,2048]{1,0:T(8,128)(2,1)S(1)}, u32[]{:S(2)}, u32[]{:S(2)}) collective-permute-start(bf16[24,2048]{1,0:T(8,128)(2,1)S(1)} %get-tuple-element.8), channel_id=1, source_target_pairs={{0,4},{1,5},{2,6},{3,7},{4,0},{5,1},{6,2},{7,3},{8,12},{9,13},{10,... | collective-permute-start | bytes 294920 | tf_op jit(solution)/shard_map/ppermute | solution.py:29
  35.6 15.5 %collective-permute-start.12 = (bf16[24,2048]{1,0:T(8,128)(2,1)S(1)}, bf16[24,2048]{1,0:T(8,128)(2,1)S(1)}, u32[]{:S(2)}, u32[]{:S(2)}) collective-permute-start(bf16[24,2048]{1,0:T(8,128)(2,1)S(1)} %get-tuple-element.8), channel_id=1, source_target_pairs={{0,12},{1,13},{2,14},{3,15},{4,8},{5,9},{6,10},{7,11},{8,4},{9,5},... | collective-permute-start | bytes 294920 | tf_op jit(solution)/shard_map/ppermute | solution.py:29
  39.4 13.4 %collective-permute-start.1 = (bf16[24,2048]{1,0:T(8,128)(2,1)S(1)}, bf16[24,2048]{1,0:T(8,128)(2,1)S(1)}, u32[]{:S(2)}, u32[]{:S(2)}) collective-permute-start(bf16[24,2048]{1,0:T(8,128)(2,1)S(1)} %get-tuple-element.6), channel_id=1, source_target_pairs={{0,8},{1,9},{2,10},{3,11},{4,12},{5,13},{6,14},{7,15},{8,0},{9,1},... | collective-permute-start | bytes 294920 | tf_op jit(solution)/shard_map/ppermute | solution.py:29
  48.5 8.4 %collective-permute-start.2 = (bf16[24,2048]{1,0:T(8,128)(2,1)S(1)}, bf16[24,2048]{1,0:T(8,128)(2,1)S(1)}, u32[]{:S(2)}, u32[]{:S(2)}) collective-permute-start(bf16[24,2048]{1,0:T(8,128)(2,1)S(1)} %get-tuple-element.6), channel_id=1, source_target_pairs={{0,4},{1,5},{2,6},{3,7},{4,0},{5,1},{6,2},{7,3},{8,12},{9,13},{10,... | collective-permute-start | bytes 294920 | tf_op jit(solution)/shard_map/ppermute | solution.py:29
  48.5 8.4 %collective-permute-start.3 = (bf16[24,2048]{1,0:T(8,128)(2,1)S(1)}, bf16[24,2048]{1,0:T(8,128)(2,1)S(1)}, u32[]{:S(2)}, u32[]{:S(2)}) collective-permute-start(bf16[24,2048]{1,0:T(8,128)(2,1)S(1)} %get-tuple-element.6), channel_id=1, source_target_pairs={{0,12},{1,13},{2,14},{3,15},{4,8},{5,9},{6,10},{7,11},{8,4},{9,5},... | collective-permute-start | bytes 294920 | tf_op jit(solution)/shard_map/ppermute | solution.py:29
  51.2 19.4 %collective-permute-start.13 = (bf16[96,2048]{1,0:T(8,128)(2,1)S(1)}, bf16[96,2048]{1,0:T(8,128)(2,1)S(1)}, u32[]{:S(2)}, u32[]{:S(2)}) collective-permute-start(bf16[96,2048]{1,0:T(8,128)(2,1)S(1)} %pad_maximum_fusion.1), channel_id=1, source_target_pairs={{0,2},{1,3},{2,0},{3,1},{4,6},{5,7},{6,4},{7,5},{8,10},{9,11},{10,... | collective-permute-start | bytes 1179656 | tf_op jit(solution)/shard_map/ppermute | solution.py:29
  56.9 13.5 %collective-permute-start.4 = (bf16[96,2048]{1,0:T(8,128)(2,1)S(1)}, bf16[96,2048]{1,0:T(8,128)(2,1)S(1)}, u32[]{:S(2)}, u32[]{:S(2)}) collective-permute-start(bf16[96,2048]{1,0:T(8,128)(2,1)S(1)} %pad_maximum_fusion), channel_id=1, source_target_pairs={{0,2},{1,3},{2,0},{3,1},{4,6},{5,7},{6,4},{7,5},{8,10},{9,11},{10,... | collective-permute-start | bytes 1179656 | tf_op jit(solution)/shard_map/ppermute | solution.py:29
  70.5 2.4 %collective-permute-start.5 = (bf16[192,2048]{1,0:T(8,128)(2,1)S(1)}, bf16[192,2048]{1,0:T(8,128)(2,1)S(1)}, u32[]{:S(2)}, u32[]{:S(2)}) collective-permute-start(bf16[192,2048]{1,0:T(8,128)(2,1)S(1)} %constant_dynamic-update-slice_fusion), channel_id=1, source_target_pairs={{0,1},{1,0},{2,3},{3,2},{4,5},{5,4},{6,7},{7,6},{8,9},{9,8},{10,11... | collective-permute-start | bytes 2359304 | tf_op jit(solution)/shard_map/ppermute | solution.py:29
  70.6 4.5 %collective-permute-start.14 = (bf16[192,2048]{1,0:T(8,128)(2,1)S(1)}, bf16[192,2048]{1,0:T(8,128)(2,1)S(1)}, u32[]{:S(2)}, u32[]{:S(2)}) collective-permute-start(bf16[192,2048]{1,0:T(8,128)(2,1)S(1)} %constant_dynamic-update-slice_fusion.5), channel_id=1, source_target_pairs={{0,1},{1,0},{2,3},{3,2},{4,5},{5,4},{6,7},{7,6},{8,9},{9,8},{10,11... | collective-permute-start | bytes 2359304 | tf_op jit(solution)/shard_map/ppermute | solution.py:29
  73.5 6.1 %collective-permute-start.6 = (f32[96,32]{0,1:T(8,128)S(1)}, f32[96,32]{0,1:T(8,128)S(1)}, u32[]{:S(2)}, u32[]{:S(2)}) collective-permute-start(f32[96,32]{0,1:T(8,128)S(1)} %get-tuple-element.34), channel_id=1, source_target_pairs={{0,2},{1,3},{2,0},{3,1},{4,6},{5,7},{6,4},{7,5},{8,10},{9,11},{10,... | collective-permute-start | bytes 36872 | tf_op jit(solution)/shard_map/ppermute | solution.py:29
  79.5 4.2 %collective-permute-start.30 = (f32[192,256]{1,0:T(8,128)S(1)}, f32[192,256]{1,0:T(8,128)S(1)}, u32[]{:S(2)}, u32[]{:S(2)}) collective-permute-start(f32[192,256]{1,0:T(8,128)S(1)} %convolution_add_fusion), channel_id=1, source_target_pairs={{0,1},{1,0},{2,3},{3,2},{4,5},{5,4},{6,7},{7,6},{8,9},{9,8},{10,11... | collective-permute-start | bytes 589832 | tf_op jit(solution)/shard_map/ppermute | solution.py:29
  79.7 3.9 %collective-permute-start.7 = (f32[48,64]{0,1:T(8,128)S(1)}, f32[48,64]{0,1:T(8,128)S(1)}, u32[]{:S(2)}, u32[]{:S(2)}) collective-permute-start(f32[48,64]{0,1:T(8,128)S(1)} %get-tuple-element.32), channel_id=1, source_target_pairs={{0,4},{1,5},{2,6},{3,7},{4,0},{5,1},{6,2},{7,3},{8,12},{9,13},{10,... | collective-permute-start | bytes 36872 | tf_op jit(solution)/shard_map/ppermute | solution.py:29
  84.0 4.7 %collective-permute-start.31 = (f32[96,256]{1,0:T(8,128)S(1)}, f32[96,256]{1,0:T(8,128)S(1)}, u32[]{:S(2)}, u32[]{:S(2)}) collective-permute-start(f32[96,256]{1,0:T(8,128)S(1)} %slice.100), channel_id=1, source_target_pairs={{0,2},{1,3},{2,0},{3,1},{4,6},{5,7},{6,4},{7,5},{8,10},{9,11},{10,... | collective-permute-start | bytes 294920 | tf_op jit(solution)/shard_map/ppermute | solution.py:29
  88.7 4.2 %collective-permute-start.32 = (f32[48,256]{1,0:T(8,128)S(1)}, f32[48,256]{1,0:T(8,128)S(1)}, u32[]{:S(2)}, u32[]{:S(2)}) collective-permute-start(f32[48,256]{1,0:T(8,128)S(1)} %slice.102), channel_id=1, source_target_pairs={{0,4},{1,5},{2,6},{3,7},{4,0},{5,1},{6,2},{7,3},{8,12},{9,13},{10,... | collective-permute-start | bytes 147464 | tf_op jit(solution)/shard_map/ppermute | solution.py:29
  89.6 4.9 %collective-permute-start.8 = (f32[24,128]{1,0:T(8,128)S(1)}, f32[24,128]{1,0:T(8,128)S(1)}, u32[]{:S(2)}, u32[]{:S(2)}) collective-permute-start(f32[24,128]{1,0:T(8,128)S(1)} %get-tuple-element.36), channel_id=1, source_target_pairs={{0,8},{1,9},{2,10},{3,11},{4,12},{5,13},{6,14},{7,15},{8,0},{9,1},... | collective-permute-start | bytes 36872 | tf_op jit(solution)/shard_map/ppermute | solution.py:29
  92.9 4.8 %collective-permute-start.33 = (f32[24,256]{1,0:T(8,128)S(1)}, f32[24,256]{1,0:T(8,128)S(1)}, u32[]{:S(2)}, u32[]{:S(2)}) collective-permute-start(f32[24,256]{1,0:T(8,128)S(1)} %slice.104), channel_id=1, source_target_pairs={{0,8},{1,9},{2,10},{3,11},{4,12},{5,13},{6,14},{7,15},{8,0},{9,1},... | collective-permute-start | bytes 73736 | tf_op jit(solution)/shard_map/ppermute | solution.py:29
  (10 other events, 150.9 us)
